TPU v7x, 32 devices: a whole 2x2x4 slice. The times are simulated.
32 devices in a mesh: clip: 4 (over z), tile: 8 (over y, x, core).
Axes of the slice: x: 2, y: 2, z: 4, core: 2. Of those that a mesh axis runs over, the one named last changes fastest.
Arguments:
- tokens: bfloat16 [256, 16, 16, 1024], P('tile', 'clip'), may hold values from -6 to 6
- mask_bits: int32 [256, 16, 16], P('tile', 'clip'), may hold values from 0 to 1, as said below
- action_ids: int32 [16, 16], P('clip'), may hold values from 0 to 7
- vectors: float32 [8, 1024], replicated, as said below
- action_table: float32 [8, 1024], replicated, may hold values from -4 to 4
- w_space_qkv: bfloat16 [1024, 3072], replicated, may hold values from -0.1875 to 0.1875
- w_space_out: bfloat16 [1024, 1024], replicated, may hold values from -1.5 to 1.5
- w_time_qkv: bfloat16 [1024, 3072], replicated, may hold values from -0.1875 to 0.1875
- w_time_out: bfloat16 [1024, 1024], replicated, may hold values from -0.5 to 0.5
- w_up: bfloat16 [1024, 4096], replicated, may hold values from -0.1875 to 0.1875
- b_up: float32 [4096], replicated, may hold values from -3 to 3
- w_down: bfloat16 [4096, 1024], replicated, may hold values from -0.09375 to 0.09375
- cotangent: bfloat16 [256, 16, 16, 1024], P('tile', 'clip'), may hold values from -6 to 6
Outputs:
- result: bfloat16 [256, 16, 16, 1024], P('tile', 'clip')
- input_grad: bfloat16 [256, 16, 16, 1024], P('tile', 'clip')
- vectors_grad: float32 [8, 1024], replicated
- table_grad: float32 [8, 1024], replicated
- space_qkv_grad: float32 [1024, 3072], P(('clip', 'tile'))
- space_out_grad: float32 [1024, 1024], P(('clip', 'tile'))
- time_qkv_grad: float32 [1024, 3072], P(('clip', 'tile'))
- time_out_grad: float32 [1024, 1024], P(('clip', 'tile'))
- up_grad: float32 [1024, 4096], P(('clip', 'tile'))
- bias_up_grad: float32 [4096], replicated
- down_grad: float32 [4096, 1024], P(('clip', 'tile'))
Inputs may be any that keep to these rules, and one draw needn't show every extreme that they name: `mask_bits`: each clip draws a share between one half and one; each of its tokens is 1 with that probability. `vectors`: gains near one, shifts and biases of a few tenths, the mask embedding of order one.
All inputs are finite; a program needn't handle non-finite values.
Results may differ from a plain program's by a relative error of at most 0.017.
Values may be sent and summed in bfloat16 or wider, within the bound.
No kernel may reach another device: no remote copies, remote signals or barrier semaphores. Data moves between devices by JAX's collectives and lax.ppermute only.
A program may use at most 576 MiB of HBM per device.

v0:
```python
from functools import partial

import jax
import jax.numpy as jnp
from jax import lax
from jax.sharding import PartitionSpec as P

HEADS = 16
HEAD_DIM = 64


EPSILON = 1e-05
NEGATIVE = -1e30


def norm_rows(values, gain_row, shift_row):
    average = jnp.mean(values, -1, keepdims=True)
    centred = values - average
    variance = jnp.mean(centred * centred, -1, keepdims=True)
    return centred * lax.rsqrt(variance + EPSILON) * gain_row + shift_row


def norm_back(values, gain_row, shift_row, upstream):
    outcome, pullback = jax.vjp(norm_rows, values, gain_row, shift_row)
    grad_values, grad_gain, grad_shift = pullback(upstream)
    return (
        grad_values,
        jnp.sum(grad_gain.reshape(-1, values.shape[-1]), 0),
        jnp.sum(grad_shift.reshape(-1, values.shape[-1]), 0),
    )


def forward_mat(left_side, right_side):
    return jnp.dot(left_side, right_side, preferred_element_type=jnp.float32)


def through_transposed(left_side, right_side):
    return lax.dot_general(
        left_side, right_side, (((1,), (1,)), ((), ())), preferred_element_type=jnp.float32
    )


def weight_grad(left_side, right_side):
    return lax.dot_general(
        left_side, right_side, (((0,), (0,)), ((), ())), preferred_element_type=jnp.float32
    )


def to_low(values):
    return values.astype(jnp.bfloat16)


def log_total(scores):
    highest = jnp.max(scores, -1, keepdims=True)
    exp_total = jnp.sum(jnp.exp(scores - highest), -1, keepdims=True)
    return highest + jnp.log(exp_total)


def space_scores(queries, key_heads):
    return jnp.einsum(
        "gbhe,kbhe->bhgk", queries, key_heads, preferred_element_type=jnp.float32
    ) * HEAD_DIM ** (-0.5)


def time_scores(queries, key_heads):
    frame_count = queries.shape[1]
    scores = jnp.einsum(
        "nqhe,nkhe->nhqk", queries, key_heads, preferred_element_type=jnp.float32
    ) * HEAD_DIM ** (-0.5)
    allowed = lax.iota(jnp.int32, frame_count)[:, None] >= lax.iota(jnp.int32, frame_count)[None, :]
    return jnp.where(allowed, scores, NEGATIVE)


def score_grads(shares, grad_shares):
    row_inner = jnp.sum(shares * grad_shares, -1, keepdims=True)
    return to_low(shares * (grad_shares - row_inner))


def split_heads(packed, lead_one, lead_two):
    return packed.reshape(lead_one, lead_two, HEADS, HEAD_DIM)


def body(
    tokens,
    mask_bits,
    action_ids,
    vectors,
    action_table,
    w_space_qkv,
    w_space_out,
    w_time_qkv,
    w_time_out,
    w_up,
    b_up,
    w_down,
    cotangent,
):
    tile_rows, clip_count, frame_count, model_width = tokens.shape
    batch_rows = clip_count * frame_count
    row_count = tile_rows * batch_rows
    sequences = tile_rows * clip_count
    score_scale = HEAD_DIM ** (-0.5)
    masked = (mask_bits > 0)[..., None]
    onehot = (action_ids[..., None] == lax.iota(jnp.int32, action_table.shape[0])).astype(
        jnp.float32
    )
    action_rows = jnp.einsum("cfa,ad->cfd", onehot, action_table, precision=lax.Precision.HIGHEST)
    embedded = jnp.where(masked, vectors[7], tokens.astype(jnp.float32)) + action_rows[None]
    embedded = embedded.reshape(row_count, model_width)
    normed_one = to_low(norm_rows(embedded, vectors[0], vectors[1]))
    packed_one = to_low(forward_mat(normed_one, w_space_qkv)).reshape(
        tile_rows, batch_rows, 3 * model_width
    )
    queries_one = split_heads(packed_one[..., :model_width], tile_rows, batch_rows)
    keyvals = packed_one[..., model_width:]
    gathered = lax.all_gather(keyvals, "tile", axis=0, tiled=True)
    full_rows = gathered.shape[0]
    scores_one = space_scores(
        queries_one, split_heads(gathered[..., :model_width], full_rows, batch_rows)
    )
    total_one = log_total(scores_one)
    shares_one = to_low(jnp.exp(scores_one - total_one))
    values_all = split_heads(gathered[..., model_width:], full_rows, batch_rows)
    blended_one = to_low(
        jnp.einsum("bhgk,kbhe->gbhe", shares_one, values_all, preferred_element_type=jnp.float32)
    ).reshape(row_count, model_width)
    after_space = embedded + forward_mat(blended_one, w_space_out)
    normed_two = to_low(norm_rows(after_space, vectors[2], vectors[3]))
    packed_two = to_low(forward_mat(normed_two, w_time_qkv)).reshape(
        sequences, frame_count, 3 * model_width
    )
    queries_two = split_heads(packed_two[..., :model_width], sequences, frame_count)
    keys_two = split_heads(packed_two[..., model_width : 2 * model_width], sequences, frame_count)
    values_two = split_heads(packed_two[..., 2 * model_width :], sequences, frame_count)
    scores_two = time_scores(queries_two, keys_two)
    total_two = log_total(scores_two)
    shares_two = to_low(jnp.exp(scores_two - total_two))
    blended_two = to_low(
        jnp.einsum("nhqk,nkhe->nqhe", shares_two, values_two, preferred_element_type=jnp.float32)
    ).reshape(row_count, model_width)
    after_time = after_space + forward_mat(blended_two, w_time_out)
    normed_three = to_low(norm_rows(after_time, vectors[4], vectors[5]))
    hidden = forward_mat(normed_three, w_up) + b_up
    active = to_low(jax.nn.gelu(hidden, approximate=True))
    result = after_time + forward_mat(active, w_down) + vectors[6]
    upstream = cotangent.astype(jnp.float32).reshape(row_count, model_width)
    upstream_low = to_low(upstream)
    grad_down = weight_grad(active, upstream_low)
    grad_active = through_transposed(upstream_low, w_down)
    outcome, gelu_back = jax.vjp(partial(jax.nn.gelu, approximate=True), hidden)
    grad_hidden = gelu_back(grad_active)[0]
    grad_bias_up = jnp.sum(grad_hidden, 0)
    grad_hidden_low = to_low(grad_hidden)
    grad_up = weight_grad(normed_three, grad_hidden_low)
    grad_normed = through_transposed(grad_hidden_low, w_up)
    grad_inner, gain_three, shift_three = norm_back(after_time, vectors[4], vectors[5], grad_normed)
    stream = upstream + grad_inner
    stream_low = to_low(stream)
    grad_time_out = weight_grad(blended_two, stream_low)
    grad_blended = to_low(through_transposed(stream_low, w_time_out)).reshape(
        sequences, frame_count, HEADS, HEAD_DIM
    )
    shares_back = jnp.exp(time_scores(queries_two, keys_two) - total_two)
    shares_low = to_low(shares_back)
    grad_values = jnp.einsum(
        "nhqk,nqhe->nkhe", shares_low, grad_blended, preferred_element_type=jnp.float32
    )
    grad_shares = jnp.einsum(
        "nqhe,nkhe->nhqk", grad_blended, values_two, preferred_element_type=jnp.float32
    )
    grad_scores = score_grads(shares_back, grad_shares)
    grad_queries = (
        jnp.einsum("nhqk,nkhe->nqhe", grad_scores, keys_two, preferred_element_type=jnp.float32)
        * score_scale
    )
    grad_keys = (
        jnp.einsum("nhqk,nqhe->nkhe", grad_scores, queries_two, preferred_element_type=jnp.float32)
        * score_scale
    )
    grad_packed = to_low(
        jnp.concatenate(
            [
                grad_queries.reshape(row_count, model_width),
                grad_keys.reshape(row_count, model_width),
                grad_values.reshape(row_count, model_width),
            ],
            -1,
        )
    )
    grad_time_qkv = weight_grad(normed_two, grad_packed)
    grad_inner, gain_two, shift_two = norm_back(
        after_space, vectors[2], vectors[3], through_transposed(grad_packed, w_time_qkv)
    )
    stream = stream + grad_inner
    stream_low = to_low(stream)
    grad_space_out = weight_grad(blended_one, stream_low)
    grad_mixed_rows = to_low(through_transposed(stream_low, w_space_out))
    grad_mixed = grad_mixed_rows.reshape(tile_rows, batch_rows, HEADS, HEAD_DIM)
    regathered = lax.all_gather(keyvals, "tile", axis=0, tiled=True)
    keys_back = split_heads(regathered[..., :model_width], full_rows, batch_rows)
    values_back = split_heads(regathered[..., model_width:], full_rows, batch_rows)
    space_shares = jnp.exp(space_scores(queries_one, keys_back) - total_one)
    space_low = to_low(space_shares)
    grad_space_shares = jnp.einsum(
        "gbhe,kbhe->bhgk", grad_mixed, values_back, preferred_element_type=jnp.float32
    )
    grad_space_scores = score_grads(space_shares, grad_space_shares)
    grad_space_queries = (
        jnp.einsum(
            "bhgk,kbhe->gbhe", grad_space_scores, keys_back, preferred_element_type=jnp.float32
        )
        * score_scale
    )
    row_total = tile_rows * lax.axis_size("tile")
    grad_key_part = (
        jnp.einsum(
            "bhgk,gbhe->kbhe", grad_space_scores, queries_one, preferred_element_type=jnp.float32
        )
        * score_scale
    )
    grad_value_part = jnp.einsum(
        "bhgk,gbhe->kbhe", space_low, grad_mixed, preferred_element_type=jnp.float32
    )
    grad_keyvals = lax.psum_scatter(
        jnp.concatenate(
            [
                grad_key_part.reshape(row_total, batch_rows, model_width),
                grad_value_part.reshape(row_total, batch_rows, model_width),
            ],
            -1,
        ).astype(jnp.bfloat16),
        "tile",
        scatter_dimension=0,
        tiled=True,
    ).astype(jnp.float32)
    grad_packed = to_low(
        jnp.concatenate(
            [grad_space_queries.reshape(tile_rows, batch_rows, model_width), grad_keyvals], -1
        ).reshape(row_count, 3 * model_width)
    )
    grad_space_qkv = weight_grad(normed_one, grad_packed)
    grad_inner, gain_one, shift_one = norm_back(
        embedded, vectors[0], vectors[1], through_transposed(grad_packed, w_space_qkv)
    )
    stream = (stream + grad_inner).reshape(tile_rows, clip_count, frame_count, model_width)
    input_grad = jnp.where(masked, 0.0, stream).astype(jnp.bfloat16)
    grad_mask = jnp.sum(jnp.where(masked, stream, 0.0), (0, 1, 2))
    grad_table = jnp.einsum(
        "cfa,cfd->ad", onehot, jnp.sum(stream, 0), precision=lax.Precision.HIGHEST
    )
    grad_vectors = jnp.stack(
        [
            gain_one,
            shift_one,
            gain_two,
            shift_two,
            gain_three,
            shift_three,
            jnp.sum(upstream, 0),
            grad_mask,
        ]
    )
    grad_vectors, grad_bias_up, grad_table = lax.psum(
        (grad_vectors, grad_bias_up, grad_table), ("clip", "tile")
    )
    space_qkv_sum, space_out_sum, time_qkv_sum, time_out_sum, summed_up, summed_down = (
        lax.psum_scatter(grad_space_qkv, ("clip", "tile"), scatter_dimension=0, tiled=True),
        lax.psum_scatter(grad_space_out, ("clip", "tile"), scatter_dimension=0, tiled=True),
        lax.psum_scatter(grad_time_qkv, ("clip", "tile"), scatter_dimension=0, tiled=True),
        lax.psum_scatter(grad_time_out, ("clip", "tile"), scatter_dimension=0, tiled=True),
        lax.psum_scatter(grad_up, ("clip", "tile"), scatter_dimension=0, tiled=True),
        lax.psum_scatter(grad_down, ("clip", "tile"), scatter_dimension=0, tiled=True),
    )
    result = result.reshape(tile_rows, clip_count, frame_count, model_width).astype(jnp.bfloat16)
    return (
        result,
        input_grad,
        grad_vectors,
        grad_table,
        space_qkv_sum,
        space_out_sum,
        time_qkv_sum,
        time_out_sum,
        summed_up,
        grad_bias_up,
        summed_down,
    )


def solution(mesh):
    placed = (
        P("tile", "clip", None, None),
        P("tile", "clip", None),
        P("clip", None),
        P(),
        P(),
        P(),
        P(),
        P(),
        P(),
        P(),
        P(),
        P(),
        P("tile", "clip", None, None),
    )
    return jax.shard_map(
        body,
        mesh=mesh,
        in_specs=placed,
        out_specs=(
            P("tile", "clip", None, None),
            P("tile", "clip", None, None),
            P(),
            P(),
            P(("clip", "tile"), None),
            P(("clip", "tile"), None),
            P(("clip", "tile"), None),
            P(("clip", "tile"), None),
            P(("clip", "tile"), None),
            P(),
            P(("clip", "tile"), None),
        ),
        check_vma=False,
    )
```

profile of v0, /device:TPU:0, one launch (start us, length us, event | category | flops | bytes accessed | tf_op | source)
XLA Modules:
  0.0 2875.1 jit_solution(3614973217495480847)
XLA Ops:
  24.8 19.7 convolution_convert_fusion.2
  58.0 12.2 reshape.265
  76.8 281.7 %all-gather.2.cloned.1.call-done = bf16[256,64,2048]{2,1,0:T(8,128)(2,1)} async-done(((bf16[32,64,2048]{2,1,0:T(8,128)(2,1)}), bf16[256,64,2048]{2,1,0:T(8,128)(2,1)}) %all-gather.2.cloned.1.call-update) | async-done | bytes 67108880 | tf_op jit(solution)/shard_map/all_gather | solution.py:116
  358.6 44.0 %fusion.54 = (bf16[256,64,1024]{2,1,0:T(8,128)(2,1)}, bf16[256,64,1024]{2,1,0:T(8,128)(2,1)}) fusion(bf16[256,64,2048]{2,1,0:T(8,128)(2,1)} %all-gather.2.cloned.1.call-done), kind=kLoop, calls=%fused_computation.123 | loop fusion | bytes 134217728 | tf_op jit(solution)/shard_map/slice | solution.py:119
  402.5 45.1 %copy.64 = bf16[256,64,1024]{0,2,1:T(8,128)(2,1)} copy(bf16[256,64,1024]{2,1,0:T(8,128)(2,1)} %get-tuple-element.31) | data formatting | bytes 67108864 | tf_op jit(solution)/shard_map/slice | solution.py:119
  447.6 30.9 %multiply_reduce_fusion.1 = (f32[64,16,32]{2,1,0:T(8,128)S(1)}, f32[64,16,32,256]{3,2,1,0:T(8,128)}) fusion(bf16[256,64,16,64]{0,3,2,1:T(8,128)(2,1)} %bitcast.124, bf16[32,64,16,64]{3,2,1,0:T(8,128)(2,1)} %reshape.265), kind=kOutput, calls=%fused_computation.15 | convolution fusion | flops 1090486272 | bytes 71434240 | tf_op jit(solution)/shard_map/gbhe,kbhe->bhgk/dot_general | solution.py:60
  478.4 15.6 exponential_reduce_fusion
  494.1 45.3 %copy.63 = bf16[256,64,1024]{0,2,1:T(8,128)(2,1)} copy(bf16[256,64,1024]{2,1,0:T(8,128)(2,1)} %get-tuple-element.32) | data formatting | bytes 67108864 | tf_op jit(solution)/shard_map/slice | solution.py:123
  539.5 26.2 convert_bitcast_fusion.2
  602.7 21.7 convolution_convert_fusion.1
  640.2 13.0 copy.70
  659.8 13.0 copy.71
  701.1 13.0 copy.72
  714.1 13.7 convert_bitcast_fusion.1
  738.7 12.3 reshape.272
  766.8 35.8 %multiply_convert_fusion.2 = (bf16[2048,4096]{1,0:T(8,128)(2,1)}, f32[2048,4096]{1,0:T(8,128)}) fusion(f32[4096]{0:T(1024)S(1)} %copy-done.59, bf16[1024,4096]{1,0:T(8,128)(2,1)} %param.22, f32[2048,1024]{1,0:T(8,128)} %copy-done.6, f32[1024]{0:T(1024)S(1)} %bitcast.154, f32[1024]{0:T(1024)S(1)} %bitcast.145, f32[2048]{0:T(1024)S(1)} %fusion.42, ...), kind=kOutput, calls=%fused_computation.12 | convolution fusion | flops 17274241024 | bytes 67149824 | tf_op jit(solution)/shard_map/dot_general | solution.py:34
  802.6 48.0 %fusion.59 = (f32[4096]{0:T(1024)}, bf16[2048,4096]{1,0:T(8,128)(2,1)}) fusion(f32[2048,4096]{1,0:T(8,128)} %get-tuple-element.55, f32[4096]{0:T(1024)S(1)} %copy-done.59, bf16[2048,1024]{1,0:T(8,128)(2,1)} %bitcast_convert_fusion, bf16[4096,1024]{1,0:T(8,128)(2,1)} %param.24), kind=kOutput, calls=%fused_computation.128 | convolution fusion | flops 17364414464 | bytes 62947328 | tf_op jit(solution)/shard_map/dot_general | solution.py:38
  850.6 27.2 multiply_reduce_fusion.3
  905.7 12.8 convert_bitcast_fusion
  918.6 20.7 multiply_reduce_fusion.2
  939.3 15.1 multiply_convert_fusion.6
  954.3 13.5 fusion.29
  988.2 11.9 reshape.277
  1011.0 12.1 reshape.276
  1055.9 23.0 multiply_reduce_fusion.4
  1111.6 39.5 %multiply_reduce_fusion = (f32[64,16,32]{2,1,0:T(8,128)S(1)}, f32[64,16,32,256]{3,2,1,0:T(8,128)}) fusion(f32[64,16,32,256]{3,2,1,0:T(8,128)} %get-tuple-element.47, f32[64,16,32]{2,1,0:T(8,128)S(1)} %copy-done.14, bf16[256,64,16,64]{0,3,2,1:T(8,128)(2,1)} %bitcast.127, bf16[32,64,16,64]{3,2,1,0:T(8,128)(2,1)} %reshape.278), kind=kOutput, calls=%fused_computation.11 | convolution fusion | flops 1107263488 | bytes 105119744 | tf_op jit(solution)/shard_map/gbhe,kbhe->bhgk/dot_general | solution.py:204
  1151.1 28.7 convolution_convert_fusion
  1179.8 27.4 multiply_convert_fusion.1
  1207.3 29.4 %multiply_convert_fusion = bf16[64,16,64,256]{3,2,1,0:T(8,128)(2,1)} fusion(bf16[64,16,32,256]{3,2,1,0:T(8,128)(2,1)} %multiply_convert_fusion.1, bf16[32,64,16,64]{3,2,1,0:T(8,128)(2,1)} %reshape.265), kind=kOutput, calls=%fused_computation.1 | convolution fusion | flops 1107296256 | bytes 54525952 | tf_op jit(solution)/shard_map/bhgk,gbhe->kbhe/dot_general | solution.py:216
  1236.7 45.8 %copy.88 = bf16[256,64,1024]{2,1,0:T(8,128)(2,1)} copy(bf16[256,64,1024]{0,2,1:T(8,128)(2,1)} %bitcast.129) | data formatting | bytes 67108864 | tf_op jit(solution)/shard_map/reshape | solution.py:227
  1282.5 45.8 %copy.89 = bf16[256,64,1024]{2,1,0:T(8,128)(2,1)} copy(bf16[256,64,1024]{0,2,1:T(8,128)(2,1)} %bitcast.128) | data formatting | bytes 67108864 | tf_op jit(solution)/shard_map/reshape | solution.py:228
  1328.3 44.3 %pad_maximum_fusion = bf16[256,64,2048]{2,1,0:T(8,128)(2,1)} fusion(bf16[256,64,1024]{2,1,0:T(8,128)(2,1)} %copy.89, bf16[256,64,1024]{2,1,0:T(8,128)(2,1)} %copy.88), kind=kLoop, calls=%fused_computation | loop fusion | flops 134217728 | bytes 134217728 | tf_op jit(solution)/shard_map/concatenate | solution.py:225
  1396.5 24.1 fusion.49
  1421.4 29.1 %fusion.9 = f32[1024,4096]{1,0:T(8,128)} fusion(bf16[2048,4096]{1,0:T(8,128)(2,1)} %get-tuple-element.64, f32[2048,1024]{1,0:T(8,128)} %copy-done.6, f32[1024]{0:T(1024)S(1)} %bitcast.155, f32[1024]{0:T(1024)S(1)} %bitcast.148, f32[2048]{0:T(1024)S(1)} %copy-done.42, f32[2048]{0:T(1024)S(1)} %copy-done.33), kind=kOutput, calls=%fused_computation.50 | convolution fusion | flops 17190354944 | bytes 41967616 | tf_op jit(solution)/shard_map/dot_general | solution.py:44
  1450.5 25.3 fusion.61
  1479.4 23.1 fusion.27
  1512.7 12.1 concatenate.18
  1524.8 231.7 %reduce-scatter.8.cloned.1.call-done = bf16[32,64,2048]{2,1,0:T(8,128)(2,1)} async-done(((bf16[256,64,2048]{2,1,0:T(8,128)(2,1)}), bf16[32,64,2048]{2,1,0:T(8,128)(2,1)}) %reduce-scatter.8.cloned.1.call-update) | async-done | bytes 8388624 | tf_op jit(solution)/shard_map/reduce_scatter | solution.py:224
  1756.5 22.2 multiply_reduce_fusion.5
  1797.9 20.5 fusion.13
  1819.0 24.4 add_convert_fusion
  1848.6 51.7 %reduce-scatter.12.cloned.1.call-done = f32[32,1024]{1,0:T(8,128)} async-done(((f32[1024,1024]{1,0:T(8,128)}), f32[32,1024]{1,0:T(8,128)}) %reduce-scatter.12.cloned.1.call-update) | async-done | bytes 131088 | tf_op jit(solution)/shard_map/reduce_scatter | solution.py:268
  1900.3 139.6 %reduce-scatter.16.cloned.1.call-done = f32[32,1024]{1,0:T(8,128)} async-done(((f32[1024,1024]{1,0:T(8,128)}), f32[32,1024]{1,0:T(8,128)}) %reduce-scatter.16.cloned.1.call-update) | async-done | bytes 131088 | tf_op jit(solution)/shard_map/reduce_scatter | solution.py:270
  2039.8 158.9 %reduce-scatter.14.cloned.1.call-done = f32[32,3072]{1,0:T(8,128)} async-done(((f32[1024,3072]{1,0:T(8,128)}), f32[32,3072]{1,0:T(8,128)}) %reduce-scatter.14.cloned.1.call-update) | async-done | bytes 393232 | tf_op jit(solution)/shard_map/reduce_scatter | solution.py:269
  2198.7 185.3 %reduce-scatter.18.cloned.1.call-done = f32[32,4096]{1,0:T(8,128)} async-done(((f32[1024,4096]{1,0:T(8,128)}), f32[32,4096]{1,0:T(8,128)}) %reduce-scatter.18.cloned.1.call-update) | async-done | bytes 524304 | tf_op jit(solution)/shard_map/reduce_scatter | solution.py:271
  2384.1 186.7 %reduce-scatter.20.cloned.1.call-done = f32[128,1024]{1,0:T(8,128)} async-done(((f32[4096,1024]{1,0:T(8,128)}), f32[128,1024]{1,0:T(8,128)}) %reduce-scatter.20.cloned.1.call-update) | async-done | bytes 524304 | tf_op jit(solution)/shard_map/reduce_scatter | solution.py:272
  2570.8 129.6 %all-reduce.3.cloned.1.call-done = (f32[8,1024]{1,0:T(8,128)}, f32[8,1024]{1,0:T(8,128)}, f32[4096]{0:T(1024)}) async-done(((f32[8,1024]{1,0:T(8,128)}, f32[8,1024]{1,0:T(8,128)}, f32[4096]{0:T(1024)}), (f32[8,1024]{1,0:T(8,128)}, f32[8,1024]{1,0:T(8,128)}, f32[4096]{0:T(1024)})) %all-reduce.3.cloned.1.call-update) | async-done | bytes 81936 | tf_op jit(solution)/shard_map/psum | solution.py:263
  2700.4 163.6 %reduce-scatter.10.cloned.1.call-done = f32[32,3072]{1,0:T(8,128)} async-done(((f32[1024,3072]{1,0:T(8,128)}), f32[32,3072]{1,0:T(8,128)}) %reduce-scatter.10.cloned.1.call-update) | async-done | bytes 393232 | tf_op jit(solution)/shard_map/reduce_scatter | solution.py:267
  (209 shorter events, 344.0 us)
Async XLA Ops:
  7.2 743.7 %copy-start = (bf16[1024,1024]{1,0:T(8,128)(2,1)S(1)}, bf16[1024,1024]{1,0:T(8,128)(2,1)}, u32[]{:S(2)}) copy-start(bf16[1024,1024]{1,0:T(8,128)(2,1)} %param.21) | copy-start | bytes 6291460
  7.2 351.4 %all-gather.2.cloned.1.call-start = ((), (), s32[]{:S(2)}) async-start(), calls=%async_computation.7 | async-start | bytes 75497472 | tf_op jit(solution)/shard_map/all_gather | solution.py:116
  8.9 11.6 copy-start.36
  9.8 10.5 copy-start.17
  20.4 24.1 copy-start.25
  20.5 24.0 copy-start.23
  20.5 24.0 copy-start.27
  24.8 19.7 copy-start.15
  52.9 1703.7 %reduce-scatter.8.cloned.1.call-start = ((), (), s32[]{:S(2)}) async-start(), calls=%async_computation.8 | async-start | bytes 75497472 | tf_op jit(solution)/shard_map/reduce_scatter | solution.py:224
  494.1 45.3 %copy-start.13 = (f32[64,16,32]{2,1,0:T(8,128)}, f32[64,16,32]{2,1,0:T(8,128)S(1)}, u32[]{:S(2)}) copy-start(f32[64,16,32]{2,1,0:T(8,128)S(1)} %log_add_fusion.1) | copy-start | bytes 393220
  597.7 5.0 copy-start.45
  597.7 5.0 copy-start.52
  597.7 26.7 copy-start.29
  602.7 21.7 copy-start.38
  659.8 13.1 copy-start.19
  694.2 19.9 copy-start.9
  762.4 115.3 %copy-start.32 = (f32[2048]{0:T(1024)}, f32[2048]{0:T(1024)S(1)}, u32[]{:S(2)}) copy-start(f32[2048]{0:T(1024)S(1)} %broadcast_multiply_fusion.1) | copy-start | bytes 24580
  766.8 111.0 %copy-start.41 = (f32[2048]{0:T(1024)}, f32[2048]{0:T(1024)S(1)}, u32[]{:S(2)}) copy-start(f32[2048]{0:T(1024)S(1)} %fusion.42) | copy-start | bytes 24580
  850.6 27.2 copy-start.7
  877.8 5.5 copy-start.4
  894.0 11.7 copy-start.10
  894.0 11.7 copy-start.20
  1045.8 5.0 copy-start.12
  1045.8 7.6 copy-start.11
  1050.8 5.1 copy-start.30
  1050.8 5.1 copy-start.39
  1050.8 5.1 copy-start.46
  1055.9 23.0 copy-start.35
  1078.9 7.2 copy-start.5
  1078.9 7.2 copy-start.22
  1086.2 7.6 copy-start.58
  1100.0 11.7 copy-start.14
  1372.6 527.6 %reduce-scatter.12.cloned.1.call-start = ((), (), s32[]{:S(2)}) async-start(), calls=%async_computation.10 | async-start | bytes 4325376 | tf_op jit(solution)/shard_map/reduce_scatter | solution.py:268
  1384.2 12.3 copy-start.31
  1384.2 12.3 copy-start.40
  1384.2 12.3 copy-start.47
  1384.2 12.3 copy-start.53
  1384.2 655.6 %reduce-scatter.16.cloned.1.call-start = ((), (), s32[]{:S(2)}) async-start(), calls=%async_computation.12 | async-start | bytes 4325376 | tf_op jit(solution)/shard_map/reduce_scatter | solution.py:270
  1396.5 802.3 %reduce-scatter.14.cloned.1.call-start = ((), (), s32[]{:S(2)}) async-start(), calls=%async_computation.11 | async-start | bytes 12976128 | tf_op jit(solution)/shard_map/reduce_scatter | solution.py:269
  1420.7 963.4 %reduce-scatter.18.cloned.1.call-start = ((), (), s32[]{:S(2)}) async-start(), calls=%async_computation.13 | async-start | bytes 17301504 | tf_op jit(solution)/shard_map/reduce_scatter | solution.py:271
  1450.4 1120.3 %reduce-scatter.20.cloned.1.call-start = ((), (), s32[]{:S(2)}) async-start(), calls=%async_computation.14 | async-start | bytes 17301504 | tf_op jit(solution)/shard_map/reduce_scatter | solution.py:272
  1475.8 1224.6 %all-reduce.3.cloned.1.call-start = ((), (), s32[]{:S(2)}) async-start(), calls=%async_computation.15 | async-start | bytes 163840 | tf_op jit(solution)/shard_map/psum | solution.py:263
  1512.7 243.8 %copy-start.26 = (f32[2048]{0:T(1024)S(1)}, f32[2048]{0:T(1024)}, u32[]{:S(2)}) copy-start(f32[2048]{0:T(1024)} %copy-done.25) | copy-start | bytes 24580
  1512.7 243.8 %copy-start.28 = (f32[2048]{0:T(1024)S(1)}, f32[2048]{0:T(1024)}, u32[]{:S(2)}) copy-start(f32[2048]{0:T(1024)} %copy-done.27) | copy-start | bytes 24580
  1512.7 243.8 %copy-start.37 = (f32[1,1024]{1,0:T(1,128)S(1)}, f32[1,1024]{1,0:T(1,128)}, u32[]{:S(2)}) copy-start(f32[1,1024]{1,0:T(1,128)} %copy-done.36) | copy-start | bytes 12292
  1756.5 22.3 copy-start.24
  1797.8 1066.2 %reduce-scatter.10.cloned.1.call-start = ((), (), s32[]{:S(2)}) async-start(), calls=%async_computation.9 | async-start | bytes 12976128 | tf_op jit(solution)/shard_map/reduce_scatter | solution.py:267
  1819.0 1049.1 %copy-start.1 = (bf16[1024,1024]{1,0:T(8,128)(2,1)S(1)}, bf16[1024,1024]{1,0:T(8,128)(2,1)}, u32[]{:S(2)}) copy-start(bf16[1024,1024]{1,0:T(8,128)(2,1)} %param.21) | copy-start | bytes 6291460
  (21 other events, 54.4 us)
Sparse Core Ops, SparseCore 0:
  53.0 305.5 all-gather.1
  1372.7 383.7 reduce-scatter.7
  1759.5 140.7 reduce-scatter.11
  1903.1 136.7 reduce-scatter.15
  2047.3 151.3 reduce-scatter.13
  2201.5 182.5 reduce-scatter.17
  2386.9 183.8 reduce-scatter.19
  2577.4 122.9 all-reduce.2
  2707.0 156.9 reduce-scatter.9
where the time goes:
time: 2890 us; the launch traced here: 2880 us
  waiting for transfers between devices  1530 us (53%)
  matrix products  640 us (22%)
  local copies, waits for them, and re-layouts  512 us (18%)
  other arithmetic  178 us (6%)
    all_gather x1, waiting for transfers between devices, body(): gathered = lax.all_gather(keyvals, 'tile', axis=0, tiled=True)  282 us
    reduce_scatter x1, waiting for transfers between devices, body(): lax.psum_scatter(jnp.concatenate([grad_key_part.reshape(row_total, batch_...  232 us
    reduce_scatter x1, waiting for transfers between devices, body(): lax.psum_scatter(grad_down, ('clip', 'tile'), scatter_dimension=0, tiled=...  187 us
    reduce_scatter x1, waiting for transfers between devices, body(): lax.psum_scatter(grad_up, ('clip', 'tile'), scatter_dimension=0, tiled=True)  185 us
    reduce_scatter x1, waiting for transfers between devices, body(): lax.psum_scatter(grad_space_qkv, ('clip', 'tile'), scatter_dimension=0, t...  164 us
    reduce_scatter x1, waiting for transfers between devices, body(): lax.psum_scatter(grad_time_qkv, ('clip', 'tile'), scatter_dimension=0, ti...  159 us
    reduce_scatter x1, waiting for transfers between devices, body(): lax.psum_scatter(grad_time_out, ('clip', 'tile'), scatter_dimension=0, ti...  140 us
    dot_general x6, matrix products, through_transposed(): lax.dot_general(left_side, right_side, (((1,), (1,)), ((), ())), preferre...  133 us
  transfers between devices with their start and end apart: 9, of which 9 were waited for; matrix products, arithmetic and copies ran while one was open for 9% of the time, Pallas kernels for 0%

commit v1 on v0

v1 whole, which is shorter than its diff:
```python
import jax
import jax.numpy as jnp
from jax import lax
from jax.experimental import pallas as pl
from jax.experimental.pallas import tpu as pltpu
from jax.sharding import PartitionSpec as P

HEADS = 16
HEAD_DIM = 64
PAIR = 2 * HEAD_DIM
EPSILON = 1e-05
NEGATIVE = -1e30
MASKED = 2.0**100
SEEN = 2.0**99
LOG2E = 1.4426950408889634
SCALE = HEAD_DIM**-0.5
F32 = jnp.float32
BF16 = jnp.bfloat16
VMEM_LIMIT = 60 * 1024 * 1024

NN = (((1,), (0,)), ((), ()))
NT = (((1,), (1,)), ((), ()))
TN = (((0,), (0,)), ((), ()))


def dot(left, right, form=NN):
    return lax.dot_general(left, right, form, preferred_element_type=F32)


def normalise(values):
    centred = values - jnp.mean(values, -1, keepdims=True)
    spread = lax.rsqrt(jnp.mean(centred * centred, -1, keepdims=True) + EPSILON)
    return centred * spread, spread


def norm_back(unit, spread, gain, upstream):
    scaled = upstream * gain
    return spread * (
        scaled
        - jnp.mean(scaled, -1, keepdims=True)
        - unit * jnp.mean(scaled * unit, -1, keepdims=True)
    )


def half_masks():
    lane = lax.broadcasted_iota(jnp.int32, (1, PAIR), 1)
    low = (lane < HEAD_DIM).astype(F32).astype(BF16)
    high = (lane >= HEAD_DIM).astype(F32).astype(BF16)
    return low, high


def attend_forward(packed, rows, width, out, total, bias):
    masks = half_masks()
    count = rows.stop - rows.start
    lane = lax.broadcasted_iota(jnp.int32, (1, PAIR), 1)
    sums = jnp.zeros((count, PAIR), F32)
    for pair in range(width // PAIR):
        at = pair * PAIR
        queries = packed[rows, at : at + PAIR]
        keys = packed[rows, width + at : width + at + PAIR]
        values = packed[rows, 2 * width + at : 2 * width + at + PAIR]
        blended = []
        for side in range(2):
            scores = dot(queries * masks[side], keys, NT) * (SCALE * LOG2E)
            if bias is not None:
                scores = scores + bias
            highest = jnp.max(scores, -1, keepdims=True)
            shares = jnp.exp2(scores - highest)
            weight = jnp.sum(shares, -1, keepdims=True)
            blended.append(dot(shares.astype(BF16), values) * (1.0 / weight))
            sums = jnp.where(lane == 2 * pair + side, highest + jnp.log2(weight), sums)
        out[rows, at : at + PAIR] = jnp.where(lane < HEAD_DIM, blended[0], blended[1]).astype(BF16)
    total[rows, :] = sums


def attend_back(packed, rows, width, grad_out, total, bias, out):
    masks = half_masks()
    for pair in range(width // PAIR):
        at = pair * PAIR
        queries = packed[rows, at : at + PAIR]
        keys = packed[rows, width + at : width + at + PAIR]
        values = packed[rows, 2 * width + at : 2 * width + at + PAIR]
        upstream = grad_out[rows, at : at + PAIR]
        grad_q = grad_k = grad_v = 0.0
        for side in range(2):
            own_q = queries * masks[side]
            own_k = keys * masks[side]
            own_up = upstream * masks[side]
            head = 2 * pair + side
            scores = dot(own_q, keys, NT) * (SCALE * LOG2E)
            if bias is not None:
                scores = scores + bias
            shares = jnp.exp2(scores - total[rows, head : head + 1])
            grad_shares = dot(own_up, values, NT)
            weighted = shares * grad_shares
            inner = jnp.sum(weighted, -1, keepdims=True)
            grad_scores = (weighted - shares * inner).astype(BF16)
            grad_q += dot(grad_scores, own_k)
            grad_k += dot(grad_scores, own_q, TN)
            grad_v += dot(shares.astype(BF16), own_up, TN)
        out[rows, at : at + PAIR] = (grad_q * SCALE).astype(BF16)
        out[rows, width + at : width + at + PAIR] = (grad_k * SCALE).astype(BF16)
        out[rows, 2 * width + at : 2 * width + at + PAIR] = grad_v.astype(BF16)


def embed(raw, vectors, actions):
    raw = raw.astype(F32)
    masked = raw > SEEN
    return jnp.where(masked, vectors[7:8, :], raw) + actions, masked


def space_forward_kernel(x, act, vectors, w_qkv, packed, out, total):
    width = x.shape[-1]
    embedded, _ = embed(x[0], vectors, act[0])
    unit, _ = normalise(embedded)
    normed = (unit * vectors[0:1, :] + vectors[1:2, :]).astype(BF16)
    packed[0] = dot(normed, w_qkv[...]).astype(BF16)
    rows = slice(0, x.shape[1])
    attend_forward(packed.at[0], rows, width, out.at[0], total.at[0], None)


def time_forward_kernel(
    sub, x, o1, act, perm, bias, vectors, w_space_out, w_qkv, w_out, h1, h2, a2, packed, o2, total
):
    frames, places, width = x.shape
    count = frames * places
    raw = dot(perm[...], x[...].reshape(count, width))
    blended = dot(perm[...], o1[...].reshape(count, width)).astype(BF16)
    actions = jnp.broadcast_to(act[...][None], (places, frames, width)).reshape(count, width)
    embedded, _ = embed(raw, vectors, actions)
    after_space = embedded + dot(blended, w_space_out[...])
    h1[...] = after_space
    unit, _ = normalise(after_space)
    normed = (unit * vectors[2:3, :] + vectors[3:4, :]).astype(BF16)
    a2[...] = normed
    packed[...] = dot(normed, w_qkv[...]).astype(BF16)
    for start in range(0, count, sub):
        attend_forward(packed, slice(start, start + sub), width, o2, total, bias[...])
    h2[...] = after_space + dot(o2[...], w_out[...])


def feed_kernel(
    tile, h2, cot, vectors, b_up, w_up, w_down, result, z, dur, a3, r2, sums, bias_grad
):
    @pl.when(pl.program_id(0) == 0)
    def _():
        sums[...] = jnp.zeros_like(sums)
        bias_grad[...] = jnp.zeros_like(bias_grad)

    after = h2[...]
    unit, spread = normalise(after)
    gain = vectors[4:5, :]
    normed = (unit * gain + vectors[5:6, :]).astype(BF16)
    a3[...] = normed
    upstream_low = cot[...]
    c = 0.7978845608028654
    total = after + vectors[6:7, :]
    grad_normed = jnp.zeros_like(after)
    for at in range(0, w_up.shape[1], tile):
        cols = slice(at, at + tile)
        hidden = dot(normed, w_up[:, cols]) + b_up[:, cols]
        grad_active = dot(upstream_low, w_down[cols, :], NT)
        square = hidden * hidden
        gate = 0.5 * jnp.tanh(hidden * (c + (c * 0.044715) * square)) + 0.5
        active = hidden * gate
        slope = gate + active * (1.0 - gate) * (2.0 * c + (6.0 * c * 0.044715) * square)
        grad_hidden = grad_active * slope
        bias_grad[:, cols] += jnp.sum(grad_hidden, 0, keepdims=True)
        active = active.astype(BF16)
        grad_hidden = grad_hidden.astype(BF16)
        z[:, cols] = active
        dur[:, cols] = grad_hidden
        total = total + dot(active, w_down[cols, :])
        grad_normed = grad_normed + dot(grad_hidden, w_up[:, cols], NT)
    result[...] = total.astype(BF16)
    upstream = upstream_low.astype(F32)
    r2[...] = upstream + norm_back(unit, spread, gain, grad_normed)
    sums[0:1, :] += jnp.sum(grad_normed * unit, 0, keepdims=True)
    sums[1:2, :] += jnp.sum(grad_normed, 0, keepdims=True)
    sums[2:3, :] += jnp.sum(upstream, 0, keepdims=True)


def time_back_kernel(
    sub, r2, h1, packed, total, perm, bias, vectors, w_out, w_qkv, grad_packed, r2_low, r1, sums, grad_out
):
    @pl.when(pl.program_id(0) == 0)
    def _():
        sums[...] = jnp.zeros_like(sums)

    count, width = r2.shape
    stream = r2[...]
    low = stream.astype(BF16)
    r2_low[...] = low
    grad_out[...] = dot(low, w_out[...], NT).astype(BF16)
    for start in range(0, count, sub):
        attend_back(
            packed, slice(start, start + sub), width, grad_out, total, bias[...], grad_packed
        )
    grad_normed = dot(grad_packed[...], w_qkv[...], NT)
    unit, spread = normalise(h1[...])
    stream = stream + norm_back(unit, spread, vectors[2:3, :], grad_normed)
    sums[0:1, :] += jnp.sum(grad_normed * unit, 0, keepdims=True)
    sums[1:2, :] += jnp.sum(grad_normed, 0, keepdims=True)
    r1[...] = dot(perm[...], stream.astype(BF16)).astype(BF16).reshape(r1.shape)


def space_back_kernel(
    r1, x, act, packed, total, vectors, w_out, w_qkv, grad_packed, a1, input_grad, frame_sum, sums, grad_out
):
    @pl.when(pl.program_id(0) == 0)
    def _():
        sums[...] = jnp.zeros_like(sums)

    count, width = x.shape[1:]
    grad_out[...] = dot(r1[0], w_out[...], NT).astype(BF16)
    attend_back(
        packed.at[0], slice(0, count), width, grad_out, total.at[0], None, grad_packed.at[0]
    )
    grad_normed = dot(grad_packed[0], w_qkv[...], NT)
    embedded, masked = embed(x[0], vectors, act[0])
    unit, spread = normalise(embedded)
    gain = vectors[0:1, :]
    a1[0] = (unit * gain + vectors[1:2, :]).astype(BF16)
    stream = r1[0].astype(F32) + norm_back(unit, spread, gain, grad_normed)
    kept = jnp.where(masked, 0.0, stream)
    input_grad[0] = kept.astype(BF16)
    whole_sum = jnp.sum(stream, 0, keepdims=True)
    frame_sum[0] = whole_sum
    sums[0:1, :] += jnp.sum(grad_normed * unit, 0, keepdims=True)
    sums[1:2, :] += jnp.sum(grad_normed, 0, keepdims=True)
    sums[2:3, :] += whole_sum - jnp.sum(kept, 0, keepdims=True)


def whole(array):
    rank = len(array.shape)
    return pl.BlockSpec(array.shape, lambda *_: (0,) * rank, pipeline_mode=pl.Buffered(1))


def struct(shape, kind):
    return jax.ShapeDtypeStruct(shape, kind)


def call(kernel, grid, operands, outs, scratch=(), flops=0):
    in_specs = [
        whole(array) if block is None else pl.BlockSpec(block, index)
        for array, block, index in operands
    ]
    out_specs = [
        pl.BlockSpec(shape, lambda *_, rank=len(shape): (0,) * rank)
        if block is None
        else pl.BlockSpec(block, index)
        for shape, _, block, index in outs
    ]
    moved = sum(a.size * a.dtype.itemsize for a, _, _ in operands)
    return pl.pallas_call(
        kernel,
        grid=grid,
        in_specs=in_specs,
        out_specs=out_specs,
        out_shape=[struct(shape, kind) for shape, kind, _, _ in outs],
        scratch_shapes=scratch,
        cost_estimate=pl.CostEstimate(flops=flops, bytes_accessed=2 * moved, transcendentals=0),
        compiler_params=pltpu.CompilerParams(vmem_limit_bytes=VMEM_LIMIT),
    )(*[a for a, _, _ in operands])


def weight_grad_kernel(left, right, out):
    out[...] = dot(left[...], right[...], TN).astype(out.dtype)


def weight_grad(left, right, tile=512):
    depth, height = left.shape
    width = right.shape[1]
    flops = 2 * depth * height * width
    if height > width:
        operands = [(left, (depth, tile), lambda i: (0, i)), (right, None, None)]
        out = [((height, width), BF16, (tile, width), lambda i: (i, 0))]
        steps = height // tile
    else:
        operands = [(left, None, None), (right, (depth, tile), lambda i: (0, i))]
        out = [((height, width), BF16, (height, tile), lambda i: (0, i))]
        steps = width // tile
    return call(weight_grad_kernel, (steps,), operands, out, flops=flops)[0]


def body(
    tokens,
    mask_bits,
    action_ids,
    vectors,
    action_table,
    w_space_qkv,
    w_space_out,
    w_time_qkv,
    w_time_out,
    w_up,
    b_up,
    w_down,
    cotangent,
):
    p, clips, frames, width = tokens.shape
    n = lax.axis_size("tile")
    me = lax.axis_index("tile")
    group = n // clips
    own_frames = frames // group
    grid_all = n * p
    places = grid_all // group
    clip, part = me // group, me % group
    hidden = w_up.shape[1]
    rows = places * frames

    def swap(value, k):
        return lax.ppermute(value, "tile", [(i, i ^ k) for i in range(n)])

    def row_block(*shape):
        return shape, lambda i: (i,) + (0,) * (len(shape) - 1)

    order = [k for j in range(group) for k in range(j, n, group)]
    onehot = (action_ids[..., None] == lax.iota(jnp.int32, action_table.shape[0])).astype(F32)
    action_rows = jnp.einsum("cfa,ad->cfd", onehot, action_table, precision=lax.Precision.HIGHEST)
    act_time = lax.dynamic_index_in_dim(action_rows, clip, 0, keepdims=False)
    act_space = lax.dynamic_slice_in_dim(act_time, part * own_frames, own_frames, 0)[:, None, :]

    marked = jnp.where((mask_bits > 0)[..., None], jnp.asarray(MASKED, BF16), tokens)
    marked = marked.reshape(p, n, own_frames, width)
    pieces = []
    for k in order:
        piece = lax.dynamic_index_in_dim(marked, me ^ k, 1, keepdims=False).transpose(1, 0, 2)
        pieces.append(piece if k == 0 else swap(piece, k))
    x_space = jnp.concatenate(pieces, 1)

    cot_pieces = []
    for j in range(n // group):
        piece = lax.dynamic_index_in_dim(cotangent, clip ^ j, 1, keepdims=False)
        cot_pieces.append(piece if j == 0 else swap(piece, j * group))
    cot = jnp.concatenate(cot_pieces, 0).reshape(rows, width)

    head_flops = 2 * HEADS * HEAD_DIM
    frame_block = lambda *shape: ((1,) + shape, lambda i: (i, 0, 0))
    packed_one, o1, total_one = call(
        space_forward_kernel,
        (own_frames,),
        [
            (x_space, *frame_block(grid_all, width)),
            (act_space, *frame_block(1, width)),
            (vectors, None, None),
            (w_space_qkv, None, None),
        ],
        [
            ((own_frames, grid_all, 3 * width), BF16, *frame_block(grid_all, 3 * width)),
            ((own_frames, grid_all, width), BF16, *frame_block(grid_all, width)),
            ((own_frames, grid_all, PAIR), F32, *frame_block(grid_all, PAIR)),
        ],
        flops=2 * own_frames * grid_all * width * 3 * width
        + 8 * own_frames * grid_all * grid_all * head_flops,
    )

    def to_time(value):
        return jnp.concatenate(
            [
                value[:, :places] if j == 0 else swap(value[:, j * places : (j + 1) * places], j)
                for j in range(group)
            ],
            0,
        )

    def to_space(value):
        return jnp.concatenate(
            [
                value[:own_frames]
                if j == 0
                else swap(value[j * own_frames : (j + 1) * own_frames], j)
                for j in range(group)
            ],
            1,
        )

    x_time, o1_time = to_time(x_space), to_time(o1)

    block = 16
    count = block * frames
    sub = min(count, 128)
    index = lax.iota(jnp.int32, count)
    slot, place = index // block, index % block
    frame_of_slot = ((part ^ (slot // own_frames)) * own_frames) + slot % own_frames
    target = place * frames + frame_of_slot
    perm_back = (target[:, None] == index[None, :]).astype(BF16)
    perm = (index[:, None] == target[None, :]).astype(BF16)
    seq = lax.iota(jnp.int32, sub)
    same = (seq[:, None] // frames) == (seq[None, :] // frames)
    bias = jnp.where(same & (seq[:, None] >= seq[None, :]), 0.0, NEGATIVE).astype(F32)

    slot_block = ((frames, block, width), lambda i: (0, i, 0))
    h1, h2, a2, packed_two, o2, total_two = call(
        lambda *refs: time_forward_kernel(sub, *refs),
        (places // block,),
        [
            (x_time, *slot_block),
            (o1_time, *slot_block),
            (act_time, None, None),
            (perm, None, None),
            (bias, None, None),
            (vectors, None, None),
            (w_space_out, None, None),
            (w_time_qkv, None, None),
            (w_time_out, None, None),
        ],
        [
            ((rows, width), F32, *row_block(count, width)),
            ((rows, width), F32, *row_block(count, width)),
            ((rows, width), BF16, *row_block(count, width)),
            ((rows, 3 * width), BF16, *row_block(count, 3 * width)),
            ((rows, width), BF16, *row_block(count, width)),
            ((rows, PAIR), F32, *row_block(count, PAIR)),
        ],
        flops=2 * rows * width * 5 * width + 8 * rows * sub * head_flops,
    )

    step = min(rows, 256)
    result, z, dur, a3, r2, sums_three, bias_up = call(
        lambda *refs: feed_kernel(1024, *refs),
        (rows // step,),
        [
            (h2, *row_block(step, width)),
            (cot, *row_block(step, width)),
            (vectors, None, None),
            (b_up[None, :], None, None),
            (w_up, None, None),
            (w_down, None, None),
        ],
        [
            ((rows, width), BF16, *row_block(step, width)),
            ((rows, hidden), BF16, *row_block(step, hidden)),
            ((rows, hidden), BF16, *row_block(step, hidden)),
            ((rows, width), BF16, *row_block(step, width)),
            ((rows, width), F32, *row_block(step, width)),
            ((8, width), F32, None, None),
            ((1, hidden), F32, None, None),
        ],
        flops=8 * rows * width * hidden,
    )

    result = result.reshape(n // group, p, 1, frames, width)
    result_out = jnp.zeros(tokens.shape, BF16)
    for j in range(n // group):
        piece = result[j] if j == 0 else swap(result[j], j * group)
        result_out = lax.dynamic_update_slice_in_dim(result_out, piece, clip ^ j, 1)

    down = weight_grad(z, cot)
    up = weight_grad(a3, dur)

    grad_packed_two, r2_low, r1_time, sums_two = call(
        lambda *refs: time_back_kernel(sub, *refs),
        (places // block,),
        [
            (r2, *row_block(count, width)),
            (h1, *row_block(count, width)),
            (packed_two, *row_block(count, 3 * width)),
            (total_two, *row_block(count, PAIR)),
            (perm_back, None, None),
            (bias, None, None),
            (vectors, None, None),
            (w_time_out, None, None),
            (w_time_qkv, None, None),
        ],
        [
            ((rows, 3 * width), BF16, *row_block(count, 3 * width)),
            ((rows, width), BF16, *row_block(count, width)),
            ((frames, places, width), BF16, *slot_block),
            ((8, width), F32, None, None),
        ],
        [pltpu.VMEM((count, width), BF16)],
        flops=2 * rows * width * 4 * width + 20 * rows * sub * head_flops,
    )
    r1_space = to_space(r1_time)
    time_out = weight_grad(o2, r2_low)
    time_qkv = weight_grad(a2, grad_packed_two)

    grad_packed_one, a1, input_low, frame_sums, sums_one = call(
        space_back_kernel,
        (own_frames,),
        [
            (r1_space, *frame_block(grid_all, width)),
            (x_space, *frame_block(grid_all, width)),
            (act_space, *frame_block(1, width)),
            (packed_one, *frame_block(grid_all, 3 * width)),
            (total_one, *frame_block(grid_all, PAIR)),
            (vectors, None, None),
            (w_space_out, None, None),
            (w_space_qkv, None, None),
        ],
        [
            ((own_frames, grid_all, 3 * width), BF16, *frame_block(grid_all, 3 * width)),
            ((own_frames, grid_all, width), BF16, *frame_block(grid_all, width)),
            ((own_frames, grid_all, width), BF16, *frame_block(grid_all, width)),
            ((own_frames, 1, width), F32, *frame_block(1, width)),
            ((8, width), F32, None, None),
        ],
        [pltpu.VMEM((grid_all, width), BF16)],
        flops=2 * rows * width * 4 * width + 20 * rows * grid_all * head_flops,
    )

    input_grad = jnp.zeros((p, n, own_frames, width), BF16)
    for slot_index, k in enumerate(order):
        piece = input_low[:, slot_index * p : (slot_index + 1) * p]
        piece = piece if k == 0 else swap(piece, k)
        input_grad = lax.dynamic_update_slice_in_dim(
            input_grad, piece.transpose(1, 0, 2)[:, None], me ^ k, 1
        )
    input_grad = input_grad.reshape(tokens.shape)

    space_out = weight_grad(o1.reshape(rows, width), r1_space.reshape(rows, width))
    space_qkv = weight_grad(a1.reshape(rows, width), grad_packed_one.reshape(rows, 3 * width))

    own_hot = lax.dynamic_slice_in_dim(
        lax.dynamic_index_in_dim(onehot, clip, 0, keepdims=False), part * own_frames, own_frames, 0
    )
    grad_table = jnp.einsum("fa,fd->ad", own_hot, frame_sums[:, 0], precision=lax.Precision.HIGHEST)
    grad_vectors = jnp.concatenate(
        [sums_one[0:2], sums_two[0:2], sums_three[0:3], sums_one[2:3]], 0
    )
    small = jnp.concatenate([grad_vectors, grad_table, bias_up.reshape(-1, width)], 0)
    small = lax.psum(small, ("clip", "tile"))
    count_v, count_t = grad_vectors.shape[0], grad_table.shape[0]

    def scatter(partial):
        summed = lax.psum_scatter(partial, ("clip", "tile"), scatter_dimension=0, tiled=True)
        return summed.astype(F32)

    return (
        result_out,
        input_grad,
        small[:count_v],
        small[count_v : count_v + count_t],
        scatter(space_qkv),
        scatter(space_out),
        scatter(time_qkv),
        scatter(time_out),
        scatter(up),
        small[count_v + count_t :].reshape(hidden),
        scatter(down),
    )


def solution(mesh):
    spread = P("tile", "clip", None, None)
    rows = P(("clip", "tile"), None)
    return jax.shard_map(
        body,
        mesh=mesh,
        in_specs=(spread, P("tile", "clip", None), P("clip", None)) + (P(),) * 9 + (spread,),
        out_specs=(spread, spread, P(), P(), rows, rows, rows, rows, rows, P(), rows),
        check_vma=False,
    )
```

time: 2890 us -> 1470 us (0.51)
  waiting for transfers between devices: 1530 us -> 860 us
  matrix products: 640 us -> 1.26 us
  Pallas kernels: 0 us -> 478 us
  local copies, waits for them, and re-layouts: 512 us -> 65.6 us
  other arithmetic: 178 us -> 31.1 us
    dot_general x31 -> x1, matrix products: 639 us -> 0.96 us  [body(): jnp.einsum('fa,fd->ad', own_hot, frame_sums[:, 0], precision=lax.Precisio...]
    pallas_call x0 -> x11, Pallas kernels: none -> 478 us  [call(): pl.pallas_call(kernel, grid=grid, in_specs=in_specs, out_specs=out_specs,...]
    reduce_scatter x7 -> x6, waiting for transfers between devices: 1120 us -> 707 us  [scatter(): lax.psum_scatter(partial, ('clip', 'tile'), scatter_dimension=0, tiled=True)]
    all_gather x1 -> x0, waiting for transfers between devices: 282 us -> none  [body(): gathered = lax.all_gather(keyvals, 'tile', axis=0, tiled=True)]
    reshape x13 -> x1, local copies, waits for them, and re-layouts: 226 us -> 0.01 us  [body(): bias_up.reshape(-1, width)]
    ppermute x0 -> x23, waiting for transfers between devices: none -> 152 us  [swap(): return lax.ppermute(value, 'tile', [(i, i ^ k) for i in range(n)])]
    slice x7 -> x9, local copies, waits for them, and re-layouts: 158 us -> 16.8 us  [the longest x1 4.31 us: to_time(): value[:, :places]]
    psum x1, waiting for transfers between devices: 130 us -> 0.01 us  [body(): small = lax.psum(small, ('clip', 'tile'))]
  transfers between devices with their start and end apart: 9 -> 30, of which waited for: 9 -> 20; matrix products, arithmetic and copies ran while one was open for 9% -> 5% of each run, Pallas kernels for 0% -> 7%
where the time goes in v1:
time: 1470 us
  waiting for transfers between devices  860 us (59%)
  Pallas kernels  478 us (33%)
  local copies, waits for them, and re-layouts  65.6 us (4%)
  other arithmetic  31.1 us (2%)
  starting transfers between devices  20.6 us (1%)
    reduce_scatter x6, waiting for transfers between devices, scatter(): lax.psum_scatter(partial, ('clip', 'tile'), scatter_dimension=0, tiled=True)  707 us
    pallas_call x11, Pallas kernels, call(): pl.pallas_call(kernel, grid=grid, in_specs=in_specs, out_specs=out_specs,...  478 us
    ppermute x23, waiting for transfers between devices, swap(): return lax.ppermute(value, 'tile', [(i, i ^ k) for i in range(n)])  152 us
  transfers between devices with their start and end apart: 30, of which 20 were waited for; matrix products, arithmetic and copies ran while one was open for 5% of the time, Pallas kernels for 7%

profile of v1, /device:TPU:0, one launch (start us, length us, event | category | flops | bytes accessed | tf_op | source)
XLA Modules:
  0.0 1470.7 jit_solution(9060373763991577599)
XLA Ops:
  8.2 2.5 broadcast_select_fusion
  13.4 2.9 collective-permute-start
  22.2 2.1 collective-permute-start.4
  31.1 12.4 collective-permute-done.1
  46.2 5.2 collective-permute-done.4
  52.4 11.4 collective-permute-done.5
  66.2 34.7 %shard_map.212 = (bf16[8,256,3072]{2,1,0:T(8,128)(2,1)}, bf16[8,256,1024]{2,1,0:T(8,128)(2,1)}, f32[8,256,128]{2,1,0:T(8,128)}) custom-call(bf16[8,256,1024]{2,1,0:T(8,128)(2,1)} %constant_dynamic-update-slice_fusion.x, f32[8,1,1024]{2,1,0:T(1,128)} %broadcast_in_dim.70.act, f32[8,1024]{1,0:T(8,128)} %vectors.3, bf16[1024,3072]{1,0:T(8,128)(2,1)} %w_qkv.3), custom_call_target="tpu_custom_call" | custom-call | flops 21474836480 | bytes 21102592 | tf_op jit(solution)/shard_map/pallas_call | solution.py:255
  101.0 4.3 fusion.17
  107.7 3.0 dynamic-slice_bitcast_fusion.3
  116.7 42.1 %collective-permute-done.10 = bf16[32,16,1024]{2,1,0:T(8,128)(2,1)S(1)} collective-permute-done((bf16[32,16,1024]{2,1,0:T(8,128)(2,1)S(1)}, bf16[32,16,1024]{2,1,0:T(8,128)(2,1)S(1)}, u32[]{:S(2)}, u32[]{:S(2)}) %collective-permute-start.10) | collective-permute-done | bytes 1048608 | tf_op jit(solution)/shard_map/ppermute | solution.py:313
  160.0 2.3 pad_maximum_fusion.2
  162.3 4.0 pad_maximum_fusion.1.refs_1_
  166.4 3.5 pad_maximum_fusion.refs_0_
  169.8 104.9 %shard_map.213 = (f32[2048,1024]{1,0:T(8,128)}, f32[2048,1024]{1,0:T(8,128)}, bf16[2048,1024]{1,0:T(8,128)(2,1)}, bf16[2048,3072]{1,0:T(8,128)(2,1)}, bf16[2048,1024]{1,0:T(8,128)(2,1)}, /*index=5*/f32[2048,128]{1,0:T(8,128)}) custom-call(bf16[16,128,1024]{2,1,0:T(8,128)(2,1)} %pad_maximum_fusion.refs_0_, bf16[16,128,1024]{2,1,0:T(8,128)(2,1)} %pad_maximum_fusion.1.refs_1_, ...), custom_call_target="tpu_custom_call" | custom-call | flops 25769803776 | bytes 38338560 | tf_op jit(solution)/shard_map/pallas_call | solution.py:255
  274.8 93.9 %shard_map.214 = (bf16[2048,1024]{1,0:T(8,128)(2,1)}, bf16[2048,4096]{1,0:T(8,128)(2,1)}, bf16[2048,4096]{1,0:T(8,128)(2,1)}, bf16[2048,1024]{1,0:T(8,128)(2,1)}...) custom-call(f32[2048,1024]{1,0:T(8,128)} %get-tuple-element.37.refs_0_, ...), custom_call_target="tpu_custom_call" | custom-call | flops 68719476736 | bytes 58818560 | tf_op jit(solution)/shard_map/pallas_call | solution.py:255
  368.6 77.2 %shard_map.215 = (bf16[2048,3072]{1,0:T(8,128)(2,1)}, bf16[2048,1024]{1,0:T(8,128)(2,1)}, bf16[16,128,1024]{2,1,0:T(8,128)(2,1)}, f32[8,1024]{1,0:T(8,128)}) custom-call(f32[2048,1024]{1,0:T(8,128)} %get-tuple-element.39.refs_0_, f32[2048,1024]{1,0:T(8,128)} %get-tuple-element.40.refs_1_, bf16[2048,3072]{1,0:T(8,128)(2,1)} %get-tuple-element.41.refs_2_, ...), custom_call_target="tpu_custom_call" | custom-call | flops 27917287424 | bytes 78053376 | tf_op jit(solution)/shard_map/pallas_call | solution.py:255
  445.9 4.2 fusion.15
  452.2 2.4 collective-permute-done.15
  454.6 4.3 pad_maximum_fusion.3.r1
  458.9 67.6 %shard_map.216 = (bf16[8,256,3072]{2,1,0:T(8,128)(2,1)}, bf16[8,256,1024]{2,1,0:T(8,128)(2,1)}, bf16[8,256,1024]{2,1,0:T(8,128)(2,1)}, f32[8,1,1024]{2,1,0:T(1,128)}, f32[8,1024]{1,0:T(8,128)}) custom-call(bf16[8,256,1024]{2,1,0:T(8,128)(2,1)} %pad_maximum_fusion.3.r1, bf16[8,256,1024]{2,1,0:T(8,128)(2,1)} %constant_dynamic-update-slice_fusion.x, ...), custom_call_target="tpu_custom_call" | custom-call | flops 38654705664 | bytes 60948480 | tf_op jit(solution)/shard_map/pallas_call | solution.py:255
  529.0 1.9 concatenate.31
  530.9 8.6 shard_map.220
  539.6 8.6 shard_map.218
  548.3 18.4 %shard_map.219 = bf16[1024,3072]{1,0:T(8,128)(2,1)} custom-call(bf16[2048,1024]{1,0:T(8,128)(2,1)} %get-tuple-element.54.left, bf16[2048,3072]{1,0:T(8,128)(2,1)} %get-tuple-element.55.right), custom_call_target="tpu_custom_call" | custom-call | flops 12884901888 | bytes 33554432 | tf_op jit(solution)/shard_map/pallas_call | solution.py:255
  566.7 18.1 %shard_map.217 = bf16[1024,3072]{1,0:T(8,128)(2,1)} custom-call(bf16[2048,1024]{1,0:T(8,128)(2,1)} %bitcast.133, bf16[2048,3072]{1,0:T(8,128)(2,1)} %bitcast.132), custom_call_target="tpu_custom_call" | custom-call | flops 12884901888 | bytes 33554432 | tf_op jit(solution)/shard_map/pallas_call | solution.py:255
  584.9 22.9 %shard_map.221 = bf16[1024,4096]{1,0:T(8,128)(2,1)} custom-call(bf16[2048,1024]{1,0:T(8,128)(2,1)} %get-tuple-element.58.left, bf16[2048,4096]{1,0:T(8,128)(2,1)} %get-tuple-element.59.right), custom_call_target="tpu_custom_call" | custom-call | flops 17179869184 | bytes 41943040 | tf_op jit(solution)/shard_map/pallas_call | solution.py:255
  607.9 22.8 %shard_map.222 = bf16[4096,1024]{1,0:T(8,128)(2,1)} custom-call(bf16[2048,4096]{1,0:T(8,128)(2,1)} %get-tuple-element.60.left, bf16[2048,1024]{1,0:T(8,128)(2,1)} %bitcast.120), custom_call_target="tpu_custom_call" | custom-call | flops 17179869184 | bytes 41943040 | tf_op jit(solution)/shard_map/pallas_call | solution.py:255
  630.8 2.6 fusion.16
  637.7 21.9 %collective-permute-done.12 = bf16[32,1,16,1024]{3,2,1,0:T(8,128)(2,1)S(1)} collective-permute-done((bf16[32,1,16,1024]{3,2,1,0:T(8,128)(2,1)S(1)}, bf16[32,1,16,1024]{3,2,1,0:T(8,128)(2,1)S(1)}, u32[]{:S(2)}, u32[]{:S(2)}) %collective-permute-start.12) | collective-permute-done | bytes 1048608 | tf_op jit(solution)/shard_map/ppermute | solution.py:313
  659.8 3.2 collective-permute-done.13
  663.1 24.2 %collective-permute-done.14 = bf16[32,1,16,1024]{3,2,1,0:T(8,128)(2,1)S(1)} collective-permute-done((bf16[32,1,16,1024]{3,2,1,0:T(8,128)(2,1)S(1)}, bf16[32,1,16,1024]{3,2,1,0:T(8,128)(2,1)S(1)}, u32[]{:S(2)}, u32[]{:S(2)}) %collective-permute-start.14) | collective-permute-done | bytes 1048608 | tf_op jit(solution)/shard_map/ppermute | solution.py:313
  687.4 2.0 fusion.14
  690.7 2.6 broadcast_in_dim.74
  694.1 2.2 collective-permute-start.18
  700.5 5.6 collective-permute-done.16
  706.1 1.9 bitcast_dynamic-update-slice_fusion.5
  708.0 13.5 collective-permute-done.17
  723.4 1.9 bitcast_dynamic-update-slice_fusion.3
  725.3 1.9 bitcast_dynamic-update-slice_fusion.2
  727.2 6.3 collective-permute-done.20
  736.2 6.6 copy.38
  742.7 2.4 collective-permute-done.22
  746.3 47.5 %reduce-scatter.13.cloned.1.call-done = bf16[32,1024]{1,0:T(8,128)(2,1)} async-done(((bf16[1024,1024]{1,0:T(8,128)(2,1)}), bf16[32,1024]{1,0:T(8,128)(2,1)}) %reduce-scatter.13.cloned.1.call-update) | async-done | bytes 65552 | tf_op jit(solution)/shard_map/reduce_scatter | solution.py:527
  795.3 133.5 %reduce-scatter.9.cloned.1.call-done = bf16[32,1024]{1,0:T(8,128)(2,1)} async-done(((bf16[1024,1024]{1,0:T(8,128)(2,1)}), bf16[32,1024]{1,0:T(8,128)(2,1)}) %reduce-scatter.9.cloned.1.call-update) | async-done | bytes 65552 | tf_op jit(solution)/shard_map/reduce_scatter | solution.py:527
  930.2 114.5 %reduce-scatter.11.cloned.1.call-done = bf16[32,3072]{1,0:T(8,128)(2,1)} async-done(((bf16[1024,3072]{1,0:T(8,128)(2,1)}), bf16[32,3072]{1,0:T(8,128)(2,1)}) %reduce-scatter.11.cloned.1.call-update) | async-done | bytes 196624 | tf_op jit(solution)/shard_map/reduce_scatter | solution.py:527
  1046.4 118.5 %reduce-scatter.7.cloned.1.call-done = bf16[32,3072]{1,0:T(8,128)(2,1)} async-done(((bf16[1024,3072]{1,0:T(8,128)(2,1)}), bf16[32,3072]{1,0:T(8,128)(2,1)}) %reduce-scatter.7.cloned.1.call-update) | async-done | bytes 196624 | tf_op jit(solution)/shard_map/reduce_scatter | solution.py:527
  1166.6 148.4 %reduce-scatter.15.cloned.1.call-done = bf16[32,4096]{1,0:T(8,128)(2,1)} async-done(((bf16[1024,4096]{1,0:T(8,128)(2,1)}), bf16[32,4096]{1,0:T(8,128)(2,1)}) %reduce-scatter.15.cloned.1.call-update) | async-done | bytes 262160 | tf_op jit(solution)/shard_map/reduce_scatter | solution.py:527
  1316.9 145.0 %reduce-scatter.17.cloned.1.call-done = bf16[128,1024]{1,0:T(8,128)(2,1)} async-done(((bf16[4096,1024]{1,0:T(8,128)(2,1)}), bf16[128,1024]{1,0:T(8,128)(2,1)}) %reduce-scatter.17.cloned.1.call-update) | async-done | bytes 262160 | tf_op jit(solution)/shard_map/reduce_scatter | solution.py:527
  (138 shorter events, 63.5 us)
Async XLA Ops:
  7.2 18.2 %copy-start = (f32[8,1024]{1,0:T(8,128)S(1)}, f32[8,1024]{1,0:T(8,128)}, u32[]{:S(2)}) copy-start(f32[8,1024]{1,0:T(8,128)} %param.17) | copy-start | bytes 98308
  7.2 690.5 %all-reduce.2.cloned.1.call-start = ((), (), s32[]{:S(2)}) async-start(), calls=%async_computation.6 | async-start | bytes 196608 | tf_op jit(solution)/shard_map/psum | solution.py:523
  12.3 13.1 copy-start.15
  13.4 15.9 %collective-permute-start = (bf16[8,32,1024]{2,1,0:T(8,128)(2,1)}, bf16[8,32,1024]{2,1,0:T(8,128)(2,1)S(1)}, u32[]{:S(2)}, u32[]{:S(2)}) collective-permute-start(bf16[8,32,1024]{2,1,0:T(8,128)(2,1)} %bitcast.114), channel_id=1, source_target_pairs={{0,2},{1,3},{2,0},{3,1},{4,6},{5,7},{6,4},{7,5},{8,10},{9,11},{10,... | collective-permute-start | bytes 1572872 | tf_op jit(solution)/shard_map/ppermute | solution.py:313
  17.4 26.0 %collective-permute-start.1 = (bf16[8,32,1024]{2,1,0:T(8,128)(2,1)}, bf16[8,32,1024]{2,1,0:T(8,128)(2,1)S(1)}, u32[]{:S(2)}, u32[]{:S(2)}) collective-permute-start(bf16[8,32,1024]{2,1,0:T(8,128)(2,1)} %bitcast.113), channel_id=1, source_target_pairs={{0,4},{1,5},{2,6},{3,7},{4,0},{5,1},{6,2},{7,3},{8,12},{9,13},{10,... | collective-permute-start | bytes 1572872 | tf_op jit(solution)/shard_map/ppermute | solution.py:313
  20.1 24.3 %collective-permute-start.2 = (bf16[8,32,1024]{2,1,0:T(8,128)(2,1)}, bf16[8,32,1024]{2,1,0:T(8,128)(2,1)S(1)}, u32[]{:S(2)}, u32[]{:S(2)}) collective-permute-start(bf16[8,32,1024]{2,1,0:T(8,128)(2,1)} %bitcast.112), channel_id=1, source_target_pairs={{0,6},{1,7},{2,4},{3,5},{4,2},{5,3},{6,0},{7,1},{8,14},{9,15},{10,... | collective-permute-start | bytes 1572872 | tf_op jit(solution)/shard_map/ppermute | solution.py:313
  21.1 24.2 %collective-permute-start.3 = (bf16[8,32,1024]{2,1,0:T(8,128)(2,1)}, bf16[8,32,1024]{2,1,0:T(8,128)(2,1)S(1)}, u32[]{:S(2)}, u32[]{:S(2)}) collective-permute-start(bf16[8,32,1024]{2,1,0:T(8,128)(2,1)} %bitcast.111), channel_id=1, source_target_pairs={{0,1},{1,0},{2,3},{3,2},{4,5},{5,4},{6,7},{7,6},{8,9},{9,8},{10,11... | collective-permute-start | bytes 1572872 | tf_op jit(solution)/shard_map/ppermute | solution.py:313
  22.2 29.2 %collective-permute-start.4 = (bf16[8,32,1024]{2,1,0:T(8,128)(2,1)}, bf16[8,32,1024]{2,1,0:T(8,128)(2,1)S(1)}, u32[]{:S(2)}, u32[]{:S(2)}) collective-permute-start(bf16[8,32,1024]{2,1,0:T(8,128)(2,1)} %bitcast.110), channel_id=1, source_target_pairs={{0,3},{1,2},{2,1},{3,0},{4,7},{5,6},{6,5},{7,4},{8,11},{9,10},{10,... | collective-permute-start | bytes 1572872 | tf_op jit(solution)/shard_map/ppermute | solution.py:313
  29.3 34.5 %collective-permute-start.5 = (bf16[8,32,1024]{2,1,0:T(8,128)(2,1)S(1)}, bf16[8,32,1024]{2,1,0:T(8,128)(2,1)S(1)}, u32[]{:S(2)}, u32[]{:S(2)}) collective-permute-start(bf16[8,32,1024]{2,1,0:T(8,128)(2,1)S(1)} %bitcast.128), channel_id=1, source_target_pairs={{0,5},{1,4},{2,7},{3,6},{4,1},{5,0},{6,3},{7,2},{8,13},{9,12},{10,... | collective-permute-start | bytes 1572872 | tf_op jit(solution)/shard_map/ppermute | solution.py:313
  43.5 57.5 %copy-start.4 = (bf16[8,32,1024]{2,1,0:T(8,128)(2,1)}, bf16[8,32,1024]{2,1,0:T(8,128)(2,1)S(1)}, u32[]{:S(2)}) copy-start(bf16[8,32,1024]{2,1,0:T(8,128)(2,1)S(1)} %collective-permute-done.1) | copy-start | bytes 1572868
  43.5 21.1 %collective-permute-start.6 = (bf16[8,32,1024]{2,1,0:T(8,128)(2,1)S(1)}, bf16[8,32,1024]{2,1,0:T(8,128)(2,1)S(1)}, u32[]{:S(2)}, u32[]{:S(2)}) collective-permute-start(bf16[8,32,1024]{2,1,0:T(8,128)(2,1)S(1)} %bitcast.127), channel_id=1, source_target_pairs={{0,7},{1,6},{2,5},{3,4},{4,3},{5,2},{6,1},{7,0},{8,15},{9,14},{10,... | collective-permute-start | bytes 1572872 | tf_op jit(solution)/shard_map/ppermute | solution.py:313
  44.4 56.6 %copy-start.6 = (bf16[8,32,1024]{2,1,0:T(8,128)(2,1)}, bf16[8,32,1024]{2,1,0:T(8,128)(2,1)S(1)}, u32[]{:S(2)}) copy-start(bf16[8,32,1024]{2,1,0:T(8,128)(2,1)S(1)} %collective-permute-done.2) | copy-start | bytes 1572868
  45.3 55.7 %copy-start.8 = (bf16[8,32,1024]{2,1,0:T(8,128)(2,1)}, bf16[8,32,1024]{2,1,0:T(8,128)(2,1)S(1)}, u32[]{:S(2)}) copy-start(bf16[8,32,1024]{2,1,0:T(8,128)(2,1)S(1)} %collective-permute-done.3) | copy-start | bytes 1572868
  51.5 49.5 %copy-start.10 = (bf16[8,32,1024]{2,1,0:T(8,128)(2,1)}, bf16[8,32,1024]{2,1,0:T(8,128)(2,1)S(1)}, u32[]{:S(2)}) copy-start(bf16[8,32,1024]{2,1,0:T(8,128)(2,1)S(1)} %collective-permute-done.4) | copy-start | bytes 1572868
  64.6 0.8 copy-start.12
  101.0 5.1 copy-start.9
  101.0 5.1 copy-start.11
  101.0 5.1 copy-start.13
  105.3 57.0 %collective-permute-start.8 = (bf16[8,128,1024]{2,1,0:T(8,128)(2,1)}, bf16[8,128,1024]{2,1,0:T(8,128)(2,1)}, u32[]{:S(2)}, u32[]{:S(2)}) collective-permute-start(bf16[8,128,1024]{2,1,0:T(8,128)(2,1)} %get-tuple-element.79), channel_id=1, source_target_pairs={{0,1},{1,0},{2,3},{3,2},{4,5},{5,4},{6,7},{7,6},{8,9},{9,8},{10,11... | collective-permute-start | bytes 6291464 | tf_op jit(solution)/shard_map/ppermute | solution.py:313
  107.7 58.7 %collective-permute-start.7 = (bf16[8,128,1024]{2,1,0:T(8,128)(2,1)}, bf16[8,128,1024]{2,1,0:T(8,128)(2,1)}, u32[]{:S(2)}, u32[]{:S(2)}) collective-permute-start(bf16[8,128,1024]{2,1,0:T(8,128)(2,1)} %pad_maximum_fusion.4), channel_id=1, source_target_pairs={{0,1},{1,0},{2,3},{3,2},{4,5},{5,4},{6,7},{7,6},{8,9},{9,8},{10,11... | collective-permute-start | bytes 6291464 | tf_op jit(solution)/shard_map/ppermute | solution.py:313
  110.7 48.1 %collective-permute-start.10 = (bf16[32,16,1024]{2,1,0:T(8,128)(2,1)S(1)}, bf16[32,16,1024]{2,1,0:T(8,128)(2,1)S(1)}, u32[]{:S(2)}, u32[]{:S(2)}) collective-permute-start(bf16[32,16,1024]{2,1,0:T(8,128)(2,1)S(1)} %get-tuple-element.77), channel_id=1, source_target_pairs={{0,4},{1,5},{2,6},{3,7},{4,0},{5,1},{6,2},{7,3},{8,12},{9,13},{10,... | collective-permute-start | bytes 3145736 | tf_op jit(solution)/shard_map/ppermute | solution.py:313
  112.3 46.5 %collective-permute-start.11 = (bf16[32,16,1024]{2,1,0:T(8,128)(2,1)S(1)}, bf16[32,16,1024]{2,1,0:T(8,128)(2,1)S(1)}, u32[]{:S(2)}, u32[]{:S(2)}) collective-permute-start(bf16[32,16,1024]{2,1,0:T(8,128)(2,1)S(1)} %get-tuple-element.76), channel_id=1, source_target_pairs={{0,6},{1,7},{2,4},{3,5},{4,2},{5,3},{6,0},{7,1},{8,14},{9,15},{10,... | collective-permute-start | bytes 3145736 | tf_op jit(solution)/shard_map/ppermute | solution.py:313
  113.2 46.8 %collective-permute-start.9 = (bf16[32,16,1024]{2,1,0:T(8,128)(2,1)S(1)}, bf16[32,16,1024]{2,1,0:T(8,128)(2,1)S(1)}, u32[]{:S(2)}, u32[]{:S(2)}) collective-permute-start(bf16[32,16,1024]{2,1,0:T(8,128)(2,1)S(1)} %get-tuple-element.75), channel_id=1, source_target_pairs={{0,2},{1,3},{2,0},{3,1},{4,6},{5,7},{6,4},{7,5},{8,10},{9,11},{10,... | collective-permute-start | bytes 3145736 | tf_op jit(solution)/shard_map/ppermute | solution.py:313
  162.3 4.0 copy-start.5
  162.3 4.0 copy-start.7
  445.9 4.2 copy-start.16
  445.9 5.6 copy-start.14
  445.9 6.3 copy-start.17
  450.1 4.5 collective-permute-start.15
  530.9 262.9 %reduce-scatter.13.cloned.1.call-start = ((), (), s32[]{:S(2)}) async-start(), calls=%async_computation.10 | async-start | bytes 2162688 | tf_op jit(solution)/shard_map/reduce_scatter | solution.py:527
  539.5 389.2 %reduce-scatter.9.cloned.1.call-start = ((), (), s32[]{:S(2)}) async-start(), calls=%async_computation.8 | async-start | bytes 2162688 | tf_op jit(solution)/shard_map/reduce_scatter | solution.py:527
  548.3 496.5 %reduce-scatter.11.cloned.1.call-start = ((), (), s32[]{:S(2)}) async-start(), calls=%async_computation.9 | async-start | bytes 6488064 | tf_op jit(solution)/shard_map/reduce_scatter | solution.py:527
  566.7 598.3 %reduce-scatter.7.cloned.1.call-start = ((), (), s32[]{:S(2)}) async-start(), calls=%async_computation.7 | async-start | bytes 6488064 | tf_op jit(solution)/shard_map/reduce_scatter | solution.py:527
  584.9 730.2 %reduce-scatter.15.cloned.1.call-start = ((), (), s32[]{:S(2)}) async-start(), calls=%async_computation.11 | async-start | bytes 8650752 | tf_op jit(solution)/shard_map/reduce_scatter | solution.py:527
  607.9 854.0 %reduce-scatter.17.cloned.1.call-start = ((), (), s32[]{:S(2)}) async-start(), calls=%async_computation.12 | async-start | bytes 8650752 | tf_op jit(solution)/shard_map/reduce_scatter | solution.py:527
  633.5 26.2 %collective-permute-start.12 = (bf16[32,1,16,1024]{3,2,1,0:T(8,128)(2,1)S(1)}, bf16[32,1,16,1024]{3,2,1,0:T(8,128)(2,1)S(1)}, u32[]{:S(2)}, u32[]{:S(2)}) collective-permute-start(bf16[32,1,16,1024]{3,2,1,0:T(8,128)(2,1)S(1)} %bitcast.126), channel_id=1, source_target_pairs={{0,2},{1,3},{2,0},{3,1},{4,6},{5,7},{6,4},{7,5},{8,10},{9,11},{10,... | collective-permute-start | bytes 3145736 | tf_op jit(solution)/shard_map/ppermute | solution.py:313
  634.1 28.8 %collective-permute-start.13 = (bf16[32,1,16,1024]{3,2,1,0:T(8,128)(2,1)S(1)}, bf16[32,1,16,1024]{3,2,1,0:T(8,128)(2,1)S(1)}, u32[]{:S(2)}, u32[]{:S(2)}) collective-permute-start(bf16[32,1,16,1024]{3,2,1,0:T(8,128)(2,1)S(1)} %bitcast.125), channel_id=1, source_target_pairs={{0,4},{1,5},{2,6},{3,7},{4,0},{5,1},{6,2},{7,3},{8,12},{9,13},{10,... | collective-permute-start | bytes 3145736 | tf_op jit(solution)/shard_map/ppermute | solution.py:313
  635.6 51.6 %collective-permute-start.14 = (bf16[32,1,16,1024]{3,2,1,0:T(8,128)(2,1)S(1)}, bf16[32,1,16,1024]{3,2,1,0:T(8,128)(2,1)S(1)}, u32[]{:S(2)}, u32[]{:S(2)}) collective-permute-start(bf16[32,1,16,1024]{3,2,1,0:T(8,128)(2,1)S(1)} %bitcast.124), channel_id=1, source_target_pairs={{0,6},{1,7},{2,4},{3,5},{4,2},{5,3},{6,0},{7,1},{8,14},{9,15},{10,... | collective-permute-start | bytes 3145736 | tf_op jit(solution)/shard_map/ppermute | solution.py:313
  637.5 49.8 %copy-start.2 = (bf16[8,256,1024]{2,1,0:T(8,128)(2,1)S(1)}, bf16[8,256,1024]{2,1,0:T(8,128)(2,1)}, u32[]{:S(2)}) copy-start(bf16[8,256,1024]{2,1,0:T(8,128)(2,1)} %get-tuple-element.46) | copy-start | bytes 12582916
  687.3 5.9 copy-start.3
  689.3 16.8 %collective-permute-start.16 = (bf16[8,32,1024]{2,1,0:T(8,128)(2,1)}, bf16[8,32,1024]{2,1,0:T(8,128)(2,1)}, u32[]{:S(2)}, u32[]{:S(2)}) collective-permute-start(bf16[8,32,1024]{2,1,0:T(8,128)(2,1)} %get-tuple-element.67), channel_id=1, source_target_pairs={{0,2},{1,3},{2,0},{3,1},{4,6},{5,7},{6,4},{7,5},{8,10},{9,11},{10,... | collective-permute-start | bytes 1572872 | tf_op jit(solution)/shard_map/ppermute | solution.py:313
  694.1 27.4 %collective-permute-start.17 = (bf16[8,32,1024]{2,1,0:T(8,128)(2,1)S(1)}, bf16[8,32,1024]{2,1,0:T(8,128)(2,1)}, u32[]{:S(2)}, u32[]{:S(2)}) collective-permute-start(bf16[8,32,1024]{2,1,0:T(8,128)(2,1)S(1)} %get-tuple-element.66), channel_id=1, source_target_pairs={{0,4},{1,5},{2,6},{3,7},{4,0},{5,1},{6,2},{7,3},{8,12},{9,13},{10,... | collective-permute-start | bytes 1572872 | tf_op jit(solution)/shard_map/ppermute | solution.py:313
  694.1 29.3 %collective-permute-start.18 = (bf16[8,32,1024]{2,1,0:T(8,128)(2,1)S(1)}, bf16[8,32,1024]{2,1,0:T(8,128)(2,1)}, u32[]{:S(2)}, u32[]{:S(2)}) collective-permute-start(bf16[8,32,1024]{2,1,0:T(8,128)(2,1)S(1)} %get-tuple-element.65), channel_id=1, source_target_pairs={{0,6},{1,7},{2,4},{3,5},{4,2},{5,3},{6,0},{7,1},{8,14},{9,15},{10,... | collective-permute-start | bytes 1572872 | tf_op jit(solution)/shard_map/ppermute | solution.py:313
  696.3 29.0 %collective-permute-start.19 = (bf16[8,32,1024]{2,1,0:T(8,128)(2,1)S(1)}, bf16[8,32,1024]{2,1,0:T(8,128)(2,1)}, u32[]{:S(2)}, u32[]{:S(2)}) collective-permute-start(bf16[8,32,1024]{2,1,0:T(8,128)(2,1)S(1)} %get-tuple-element.64), channel_id=1, source_target_pairs={{0,1},{1,0},{2,3},{3,2},{4,5},{5,4},{6,7},{7,6},{8,9},{9,8},{10,11... | collective-permute-start | bytes 1572872 | tf_op jit(solution)/shard_map/ppermute | solution.py:313
  696.3 37.2 %collective-permute-start.20 = (bf16[8,32,1024]{2,1,0:T(8,128)(2,1)S(1)}, bf16[8,32,1024]{2,1,0:T(8,128)(2,1)}, u32[]{:S(2)}, u32[]{:S(2)}) collective-permute-start(bf16[8,32,1024]{2,1,0:T(8,128)(2,1)S(1)} %get-tuple-element.63), channel_id=1, source_target_pairs={{0,3},{1,2},{2,1},{3,0},{4,7},{5,6},{6,5},{7,4},{8,11},{9,10},{10,... | collective-permute-start | bytes 1572872 | tf_op jit(solution)/shard_map/ppermute | solution.py:313
  706.1 29.2 %collective-permute-start.21 = (bf16[8,32,1024]{2,1,0:T(8,128)(2,1)S(1)}, bf16[8,32,1024]{2,1,0:T(8,128)(2,1)S(1)}, u32[]{:S(2)}, u32[]{:S(2)}) collective-permute-start(bf16[8,32,1024]{2,1,0:T(8,128)(2,1)S(1)} %get-tuple-element.62), channel_id=1, source_target_pairs={{0,5},{1,4},{2,7},{3,6},{4,1},{5,0},{6,3},{7,2},{8,13},{9,12},{10,... | collective-permute-start | bytes 1572872 | tf_op jit(solution)/shard_map/ppermute | solution.py:313
  721.6 23.6 %collective-permute-start.22 = (bf16[8,32,1024]{2,1,0:T(8,128)(2,1)S(1)}, bf16[8,32,1024]{2,1,0:T(8,128)(2,1)S(1)}, u32[]{:S(2)}, u32[]{:S(2)}) collective-permute-start(bf16[8,32,1024]{2,1,0:T(8,128)(2,1)S(1)} %get-tuple-element.61), channel_id=1, source_target_pairs={{0,7},{1,6},{2,5},{3,4},{4,3},{5,2},{6,1},{7,0},{8,15},{9,14},{10,... | collective-permute-start | bytes 1572872 | tf_op jit(solution)/shard_map/ppermute | solution.py:313
  736.2 727.5 %copy-start.1 = (f32[8,1024]{1,0:T(8,128)S(1)}, f32[8,1024]{1,0:T(8,128)}, u32[]{:S(2)}) copy-start(f32[8,1024]{1,0:T(8,128)} %param.17) | copy-start | bytes 98308
Sparse Core Ops, SparseCore 0:
  531.0 120.9 all-reduce.1
  654.2 139.4 reduce-scatter.12
  796.1 132.5 reduce-scatter.8
  934.2 110.4 reduce-scatter.10
  1051.1 113.7 reduce-scatter.6
  1167.1 147.9 reduce-scatter.14
  1317.4 144.4 reduce-scatter.16
